TPU v7x, 32 devices: a whole 2x2x4 slice. The times are simulated.
32 devices in a mesh: rows: 16 (over z, y, core), diag: 2 (over x).
Axes of the slice: x: 2, y: 2, z: 4, core: 2. Of those that a mesh axis runs over, the one named last changes fastest.
Arguments:
- bins: bfloat16 [4096, 32], P('rows'), may hold values from -6 to 6
- conv_weight: bfloat16 [2, 3, 3, 32, 32], replicated, may hold values from -0.375 to 0.375
- head_weight: bfloat16 [32], replicated, may hold values from -1 to 1
- dilation: int32 [2], replicated, may hold values from 1 to 8, as said below
- tile_table: int32 [16, 8], P('rows', 'diag'), may hold values from 0 to 7, each once within a row
- cotangent: bfloat16 [16, 8, 128, 128], P('rows', 'diag'), may hold values from -0.59765625 to 0.59765625
Outputs:
- predicted: bfloat16 [16, 8, 128, 128], P('rows', 'diag')
- grad_bins: float32 [4096, 32], P(('rows', 'diag'))
- grad_conv: float32 [2, 3, 3, 32, 32], replicated
- grad_head: float32 [32], replicated
Inputs may be any that keep to these rules, and one draw needn't show every extreme that they name: `dilation`: one of the 2 dilations equals 8.
All inputs are finite; a program needn't handle non-finite values.
Results may differ from a plain program's by a relative error of at most 0.013.
The roundings to bfloat16 on the way count: a program that leaves them out, or rounds other values in their place, can miss the bound.
Values may be sent and summed in bfloat16 or wider, within the bound.
A program may use at most 128 MiB of HBM per device.

v0:
```python
from functools import partial

import jax
import jax.numpy as jnp
from jax import lax
from jax.experimental import pallas as pl
from jax.experimental.pallas import tpu as pltpu
from jax.sharding import PartitionSpec as P

TILE = 128
OFFS = 4
DMAX = 8
BAND = 384
GROUP = 8
OUTSIDE = -1e30


def shifted_2(block, axis, distance):
    devices = range(lax.axis_size(axis))
    route = [(i - distance, i) for i in devices if i - distance in devices]
    return lax.ppermute(block, axis, route)


def shifts(value, spacing, lane):
    before = jnp.where(lane >= spacing, pltpu.roll(value, spacing, 1), 0.0)
    after = jnp.where(lane < TILE - spacing, pltpu.roll(value, TILE - spacing, 1), 0.0)
    return before, value, after


def tower_kernel(
    tiles_ref, dil_ref, base_ref,
    left_ref, right_ref, cot_ref, k0_ref, k1_ref, k0t_ref, head_ref,
    pred_ref, gwin_ref, gk0_ref, u1_ref, gh_ref,
    a0_ref, a1_ref, gs_ref, cs_ref, pair_ref, pair1_ref, right3_ref, cot_f, cot_b, cot_a, pred_f,
    *, total_bins,
):
    step = pl.program_id(0)
    channels = head_ref.shape[0]
    tile_id = tiles_ref[step]
    d0 = dil_ref[0]
    d1 = dil_ref[1]
    local_row = tile_id // OFFS
    offset = tile_id % OFFS

    @pl.when(step == 0)
    def _():
        for ref in (a0_ref, a1_ref, gs_ref, cs_ref):
            edge = jnp.zeros((DMAX,) + ref.shape[1:], ref.dtype)
            ref[:DMAX] = edge
            ref[TILE + DMAX:] = edge
        for ref in (gwin_ref, gk0_ref, u1_ref, gh_ref):
            ref[...] = jnp.zeros_like(ref)

    lane = lax.broadcasted_iota(jnp.int32, (channels, TILE), 1)
    lane_t = lax.broadcasted_iota(jnp.int32, (TILE, TILE), 1)
    sub_t = lax.broadcasted_iota(jnp.int32, (TILE, TILE), 0)
    sub_c = lax.broadcasted_iota(jnp.int32, (16, TILE), 0)
    distance = offset * TILE + lane_t - sub_t
    second = (base_ref[0] + local_row + offset) * TILE + lane_t
    keep = (distance >= 0) & (distance <= BAND) & (second < total_bins)
    masked = jnp.where(keep, cot_ref[0].astype(jnp.float32), 0.0)
    before, _, after = shifts(masked, d1, lane_t)
    cot_f[...] = masked
    cot_b[...] = before
    cot_a[...] = after
    right = right_ref[0]
    right3_ref[:channels] = jnp.where(lane >= d0, pltpu.roll(right, d0, 1), OUTSIDE)
    right3_ref[channels:2 * channels] = right
    right3_ref[2 * channels:] = jnp.where(lane < TILE - d0, pltpu.roll(right, TILE - d0, 1), OUTSIDE)

    def put(ref, p, value, spacing):
        parts = [part.astype(jnp.bfloat16) for part in shifts(value, spacing, lane)]
        ref[p + DMAX] = jnp.concatenate(parts, 0)

    def column(ref, row, spacing):
        return [ref[row - spacing], ref[row], ref[row + spacing]]

    def beside(columns):
        return jnp.concatenate([jnp.concatenate(parts, 0) for parts in columns], 1)

    def transposed_dot(x, y):
        return lax.dot_general(x, y, (((1,), (1,)), ((), ())), preferred_element_type=jnp.float32)

    def first(g, _):
        left = left_ref[0, g]
        for j in range(GROUP):
            p = g * GROUP + j
            one = jnp.broadcast_to(left[:, j:j + 1], (channels, TILE))
            pairs = 0.5 * (jnp.concatenate([one] * 3, 0) + right3_ref[...])
            pair_ref[p] = pairs[channels:2 * channels]
            a0_ref[p + DMAX] = jnp.maximum(pairs, 0.0).astype(jnp.bfloat16)
            row = jnp.where(
                sub_c == 0, cot_b[pl.ds(p, 1), :],
                jnp.where(sub_c == 1, cot_f[pl.ds(p, 1), :],
                          jnp.where(sub_c == 2, cot_a[pl.ds(p, 1), :], 0.0)))
            cs_ref[p + DMAX] = row.astype(jnp.bfloat16)
        return 0

    lax.fori_loop(0, TILE // GROUP, first, 0)

    def second_layer(g, _):
        for j in range(0, GROUP, 2):
            p = g * GROUP + j
            at = p + DMAX
            around = beside([column(a0_ref, at + i, d0) for i in range(2)])
            out = jnp.dot(k0_ref[...], around, preferred_element_type=jnp.float32)
            for i in range(2):
                value = pair_ref[p + i] + out[:, i * TILE:(i + 1) * TILE]
                pair1_ref[p + i] = value
                put(a1_ref, p + i, jnp.maximum(value, 0.0), d1)
        return 0

    lax.fori_loop(0, TILE // GROUP, second_layer, 0)

    head = head_ref[...]

    def turn(g, carry):
        acc_u, acc_h = carry
        base = g * GROUP
        rows = []
        for j in range(0, GROUP, 2):
            p = base + j
            at = p + DMAX
            around = beside([column(a1_ref, at + i, d1) + column(cs_ref, at + i, d1) for i in range(2)])
            out = jnp.dot(k1_ref[...], around, preferred_element_type=jnp.float32)
            for i in range(2):
                value = pair1_ref[p + i]
                cot = cot_f[pl.ds(p + i, 1), :]
                pair2 = value + out[:channels, i * TILE:(i + 1) * TILE]
                rows.append(jnp.sum(head * pair2, 0, keepdims=True))
                acc_h = acc_h + pair2 * cot
                grad = head * cot + jnp.where(value > 0.0, out[channels:, i * TILE:(i + 1) * TILE], 0.0)
                pair_ref[p + i] = grad
                put(gs_ref, p + i, grad, d0)
        pred_f[pl.ds(pl.multiple_of(base, GROUP), GROUP), :] = jnp.concatenate(rows, 0)
        every = [base + DMAX + j for j in range(GROUP)]
        acc_u = acc_u + transposed_dot(
            beside([[a1_ref[at]] for at in every]), beside([column(cs_ref, at, d1) for at in every]))
        return acc_u, acc_h

    acc_u, acc_h = lax.fori_loop(
        0, TILE // GROUP, turn, (jnp.zeros(u1_ref.shape, jnp.float32), jnp.zeros(gh_ref.shape, jnp.float32)))
    u1_ref[...] += acc_u
    gh_ref[...] += acc_h
    pred_ref[0] = pred_f[...].astype(jnp.bfloat16)
    mid = slice(channels, 2 * channels)

    def last(g, carry):
        grad_left, grad_right = carry
        base = g * GROUP
        for j in range(0, GROUP, 2):
            p = base + j
            at = p + DMAX
            around = beside([column(gs_ref, at + i, d0) for i in range(2)])
            out = jnp.dot(k0t_ref[...], around, preferred_element_type=jnp.float32)
            for i in range(2):
                active = a0_ref[at + i, mid].astype(jnp.float32) > 0.0
                grad = pair_ref[p + i] + jnp.where(active, out[:, i * TILE:(i + 1) * TILE], 0.0)
                grad_right = grad_right + grad
                grad_left = jnp.where(lane == p + i, jnp.sum(grad, 1, keepdims=True), grad_left)
        every = [base + DMAX + j for j in range(GROUP)]
        gk0_ref[...] += transposed_dot(
            beside([[a0_ref[at]] for at in every]),
            beside([[gs_ref[at - d0, mid], gs_ref[at, mid], gs_ref[at + d0, mid]] for at in every]))
        return grad_left, grad_right

    zeros = jnp.zeros((channels, TILE), jnp.float32)
    grad_left, grad_right = lax.fori_loop(0, TILE // GROUP, last, (zeros, zeros))
    gwin_ref[local_row] += 0.5 * grad_left
    gwin_ref[local_row + offset] += 0.5 * grad_right


def tower(tiles, dilation, base_row, window, conv_weight, head_weight, cotangent, total_bins, tile_rows):
    slots = tiles.shape[0]
    channels = window.shape[1]
    blocks = window.shape[0] // TILE
    bf16 = jnp.bfloat16
    f32 = jnp.float32
    window = window.astype(f32)
    left = window[:tile_rows * TILE].reshape(tile_rows, TILE // GROUP, GROUP, channels).transpose(0, 1, 3, 2)
    right = window.reshape(blocks, TILE, channels).transpose(0, 2, 1)
    width = 3 * channels
    taps = 9 * channels
    k0 = conv_weight[0].reshape(taps, channels).T
    k0t = conv_weight[0, ::-1, ::-1].transpose(2, 0, 1, 3).reshape(channels, taps)
    head_f = head_weight.astype(f32)
    folded = jnp.sum(conv_weight[1].astype(f32) * head_f, -1)[::-1, ::-1]
    w1 = jnp.pad(folded, ((0, 0), (0, 13), (0, 0))).transpose(2, 0, 1).reshape(channels, 48).astype(bf16)
    k1 = conv_weight[1].reshape(taps, channels).T
    k1 = jnp.concatenate([jnp.pad(k1, ((0, 0), (0, 48))), jnp.pad(w1, ((0, 0), (taps, 0)))], 0)
    head_b = jnp.broadcast_to(head_f[:, None], (channels, TILE))

    def whole(shape):
        return pl.BlockSpec(shape, lambda s, *_: (0,) * len(shape))

    padded = TILE + 2 * DMAX
    outs = pl.pallas_call(
        partial(tower_kernel, total_bins=total_bins),
        grid_spec=pltpu.PrefetchScalarGridSpec(
            num_scalar_prefetch=3,
            grid=(slots,),
            in_specs=[
                pl.BlockSpec((1, TILE // GROUP, channels, GROUP), lambda s, t, d, b: (t[s] // OFFS, 0, 0, 0)),
                pl.BlockSpec((1, channels, TILE), lambda s, t, d, b: (t[s] // OFFS + t[s] % OFFS, 0, 0)),
                pl.BlockSpec((1, TILE, TILE), lambda s, t, d, b: (s, 0, 0)),
                whole(k0.shape), whole(k1.shape), whole(k0t.shape), whole(head_b.shape),
            ],
            out_specs=[
                pl.BlockSpec((1, TILE, TILE), lambda s, t, d, b: (s, 0, 0)),
                whole((blocks, channels, TILE)),
                whole((3 * channels, 3 * channels)),
                whole((3 * channels, 48)),
                whole((channels, TILE)),
            ],
            scratch_shapes=[
                pltpu.VMEM((padded, width, TILE), bf16),
                pltpu.VMEM((padded, width, TILE), bf16),
                pltpu.VMEM((padded, width, TILE), bf16),
                pltpu.VMEM((padded, 16, TILE), bf16),
                pltpu.VMEM((TILE, channels, TILE), f32),
                pltpu.VMEM((TILE, channels, TILE), f32),
                pltpu.VMEM((width, TILE), f32),
                pltpu.VMEM((TILE, TILE), f32),
                pltpu.VMEM((TILE, TILE), f32),
                pltpu.VMEM((TILE, TILE), f32),
                pltpu.VMEM((TILE, TILE), f32),
            ],
        ),
        out_shape=[
            jax.ShapeDtypeStruct((slots, TILE, TILE), bf16),
            jax.ShapeDtypeStruct((blocks, channels, TILE), f32),
            jax.ShapeDtypeStruct((3 * channels, 3 * channels), f32),
            jax.ShapeDtypeStruct((3 * channels, 48), f32),
            jax.ShapeDtypeStruct((channels, TILE), f32),
        ],
        compiler_params=pltpu.CompilerParams(
            dimension_semantics=("arbitrary",), vmem_limit_bytes=40 * 1024 * 1024),
        name="tower",
    )(tiles, dilation, base_row, left, right, cotangent, k0, k1, k0t, head_b)
    return outs


def steps_of(size):
    steps, low = [], 1
    while low < size:
        span = min(4, size // low)
        steps.append([low * e for e in range(1, span)])
        low *= span
    return steps


def exchange_kernel(
    rows_n, diag_n, tile_rows, per,
    flat_ref, gwin_ref, sum_ref, bins_ref,
    part_ref, got_ref, near_ref, far_ref, own_got, near_got, far_got,
    sum_send, sum_recv, own_send, own_recv, near_send, near_recv, far_send, far_recv,
):
    g = lax.axis_index("rows")
    d = lax.axis_index("diag")
    count = bins_ref.shape[0]
    mesh_id = pl.DeviceIdType.MESH
    steps = [("rows", e) for e in steps_of(rows_n)] + [("diag", e) for e in steps_of(diag_n)]

    def start_of(index):
        return index * per // TILE

    def at(row, diag):
        return {"rows": row, "diag": diag}

    def partner(axis, e):
        return at(g ^ e, d) if axis == "rows" else at(g, d ^ e)

    barrier = pltpu.get_barrier_semaphore()

    def greet(device):
        pl.semaphore_signal(barrier, inc=1, device_id=device, device_id_type=mesh_id)

    met = 0
    for axis, group in steps:
        for e in group:
            greet(partner(axis, e))
            met += 1
    for e in range(1, diag_n):
        greet(at(g, d ^ e))
        met += 1
    firsts = sum(1 for index in range(diag_n) if index * per // TILE == 0)
    for e in range(diag_n):
        @pl.when(g >= 1)
        def _():
            greet(at(g - 1, d ^ e))

        @pl.when((g >= 2) & (start_of(d) == 0))
        def _():
            greet(at(g - 2, d ^ e))
    to_near = 1 - (g + 1) // rows_n
    to_far = 1 - (g + 2) // rows_n
    pl.semaphore_wait(barrier, met + diag_n * to_near + firsts * to_far)

    def remote(src, dst, send, recv, device):
        return pltpu.make_async_remote_copy(
            src_ref=src, dst_ref=dst, send_sem=send, recv_sem=recv,
            device_id=device, device_id_type=mesh_id)

    def sum_copy(step, slot, axis, e):
        src = flat_ref if step == 0 else part_ref.at[step - 1]
        return remote(src, got_ref.at[slot], sum_send.at[slot], sum_recv.at[slot], partner(axis, e))

    def own_copy(e):
        src = gwin_ref.at[pl.ds(start_of(d ^ e), count)]
        return remote(src, own_got.at[e - 1], own_send.at[e - 1], own_recv.at[e - 1], at(g, d ^ e))

    def near_copy(e):
        src = near_ref.at[pl.ds(start_of(d ^ e), count)]
        return remote(src, near_got.at[e], near_send.at[e], near_recv.at[e], at(g + 1, d ^ e))

    def far_copy(e):
        return remote(far_ref, far_got.at[e], far_send.at[e], far_recv.at[e], at(g + 2, d ^ e))

    sends_near = g + 1 < rows_n
    gets_near = g >= 1
    gets_far = (g >= 2) & (start_of(d) == 0)

    def sends_far(e):
        return (g + 2 < rows_n) & (start_of(d ^ e) == 0)

    near_ref[...] = gwin_ref[tile_rows:2 * tile_rows].astype(jnp.bfloat16)
    far_ref[...] = gwin_ref[2 * tile_rows].astype(jnp.bfloat16)
    slot = 0
    value = flat_ref[...]
    copies = []
    for step, (axis, group) in enumerate(steps):
        if step > 0:
            part_ref[step - 1] = value
        here = [sum_copy(step, slot + i, axis, e) for i, e in enumerate(group)]
        for copy in here:
            copy.start()
        if step == 0:
            for e in range(1, diag_n):
                own_copy(e).start()
            for e in range(diag_n):
                pl.when(sends_near)(near_copy(e).start)
                pl.when(sends_far(e))(far_copy(e).start)
        for copy in here:
            copy.wait_recv()
        others = [got_ref[slot + i] for i in range(len(group))]
        value = value + others[0]
        if len(group) == 3:
            value = value + (others[1] + others[2])
        slot += len(group)
        copies += here
    sum_ref[...] = value

    bins_ref[...] = gwin_ref[pl.ds(start_of(d), count)]
    for e in range(1, diag_n):
        own_copy(e).wait_recv()
        bins_ref[...] += own_got[e - 1]

    @pl.when(gets_near)
    def _():
        for e in range(diag_n):
            near_copy(e).wait_recv()
            bins_ref[...] += near_got[e].astype(jnp.float32)

    @pl.when(gets_far)
    def _():
        for e in range(diag_n):
            far_copy(e).wait_recv()
            bins_ref[0] += far_got[e].astype(jnp.float32)

    for copy in copies:
        copy.wait_send()
    for e in range(1, diag_n):
        own_copy(e).wait_send()
    for e in range(diag_n):
        pl.when(sends_near)(near_copy(e).wait_send)
        pl.when(sends_far(e))(far_copy(e).wait_send)


def exchange(flat, gwin, tile_rows):
    rows_n = lax.axis_size("rows")
    diag_n = lax.axis_size("diag")
    per = tile_rows * TILE // diag_n
    count = max(1, per // TILE)
    steps = steps_of(rows_n) + steps_of(diag_n)
    slots = sum(len(group) for group in steps)
    channels = gwin.shape[1]
    block = (channels, TILE)
    f32, bf16 = jnp.float32, jnp.bfloat16
    dma = pltpu.SemaphoreType.DMA
    others = max(1, diag_n - 1)
    vmem = pl.BlockSpec(memory_space=pltpu.VMEM)
    total, bins = pl.pallas_call(
        partial(exchange_kernel, rows_n, diag_n, tile_rows, per),
        out_shape=[jax.ShapeDtypeStruct(flat.shape, f32), jax.ShapeDtypeStruct((count,) + block, f32)],
        in_specs=[vmem] * 2,
        out_specs=[vmem] * 2,
        scratch_shapes=[
            pltpu.VMEM((len(steps),) + flat.shape, f32),
            pltpu.VMEM((slots,) + flat.shape, f32),
            pltpu.VMEM((tile_rows,) + block, bf16),
            pltpu.VMEM(block, bf16),
            pltpu.VMEM((others, count) + block, f32),
            pltpu.VMEM((diag_n, count) + block, bf16),
            pltpu.VMEM((diag_n,) + block, bf16),
            dma((slots,)), dma((slots,)), dma((others,)), dma((others,)),
            dma((diag_n,)), dma((diag_n,)), dma((diag_n,)), dma((diag_n,)),
        ],
        compiler_params=pltpu.CompilerParams(collective_id=0, has_side_effects=True),
        name="exchange",
    )(flat, gwin)
    bins = bins.transpose(0, 2, 1).reshape(count * TILE, channels)
    if per < TILE:
        inside = lax.axis_index("diag") * per % TILE
        bins = lax.dynamic_slice_in_dim(bins, inside, per, 0)
    return total, bins


def on_device(bins, conv_weight, head_weight, dilation, tile_table, cotangent):
    bin_dev = bins.shape[0]
    channels = bins.shape[1]
    tile_rows = bin_dev // TILE
    total_bins = lax.axis_size("rows") * bin_dev
    following = shifted_2(bins, "rows", -1)
    farther = shifted_2(bins[:TILE], "rows", -2)
    window = jnp.concatenate([bins, following, farther], 0)
    base_row = (lax.axis_index("rows") * tile_rows).astype(jnp.int32).reshape(1)
    predicted, gwin, gk0, u1, gh = tower(
        tile_table[0], dilation, base_row, window, conv_weight, head_weight, cotangent[0],
        total_bins, tile_rows)
    width = 3 * channels
    head_sum = jnp.pad(jnp.sum(gh, 1), (0, width - channels))[:, None]
    flat = jnp.concatenate([gk0, u1[:, 1::16], head_sum], 1)
    flat = jnp.pad(flat, ((0, 0), (0, TILE - flat.shape[1])))
    total, grad_bins = exchange(flat, gwin, tile_rows)
    grad_k0 = total[:, :width].reshape(3, channels, 3, channels)[:, :, ::-1].transpose(2, 0, 1, 3)
    u_sum = total[:, width:width + 3].reshape(3, channels, 3)[:, :, ::-1].transpose(2, 0, 1)
    grad_k1 = u_sum[..., None] * head_weight.astype(jnp.float32)
    grad_head = total[:channels, width + 3]
    return (predicted[None], grad_bins, jnp.stack([grad_k0, grad_k1]), grad_head)


def solution(mesh):
    in_specs = (P("rows", None), P(), P(), P(), P("rows", "diag"), P("rows", "diag", None, None))
    out_specs = (P("rows", "diag", None, None), P(("rows", "diag"), None), P(), P())
    return jax.shard_map(
        on_device, mesh=mesh, in_specs=in_specs, out_specs=out_specs, check_vma=False
    )
```

profile of v0, /device:TPU:0, one launch (start us, length us, event | category | flops | bytes accessed | tf_op | source)
XLA Modules:
  0.0 111.8 jit_solution(11278213608764572758)
XLA Ops:
  0.6 1.3 %collective-permute-start = (bf16[256,32]{0,1:T(8,128)(2,1)}, bf16[256,32]{0,1:T(8,128)(2,1)S(1)}, u32[]{:S(2)}, u32[]{:S(2)}) collective-permute-start(bf16[256,32]{0,1:T(8,128)(2,1)} %param.6), channel_id=1, source_target_pairs={{2,0},{4,2},{6,4},{8,6},{10,8},{12,10},{14,12},{16,14},{18,16},{20... | collective-permute-start | bytes 49160 | tf_op jit(solution)/shard_map/ppermute | solution.py:21
  1.9 0.7 slice.25
  2.6 1.3 %collective-permute-start.1 = (bf16[128,32]{0,1:T(8,128)(2,1)S(1)}, bf16[128,32]{0,1:T(8,128)(2,1)S(1)}, u32[]{:S(2)}, u32[]{:S(2)}) collective-permute-start(bf16[128,32]{0,1:T(8,128)(2,1)S(1)} %slice.25), channel_id=1, source_target_pairs={{4,0},{6,2},{8,4},{10,6},{12,8},{14,10},{16,12},{18,14},{20,16},{2... | collective-permute-start | bytes 24584 | tf_op jit(solution)/shard_map/ppermute | solution.py:21
  4.0 1.0 fusion.4
  4.9 0.1 fusion
  5.4 0.6 copy-done.6
  6.0 0.1 copy.16
  6.3 0.1 reshape.46.k0t_ref
  6.4 0.1 copy.17
  6.6 3.2 %collective-permute-done.1 = bf16[128,32]{0,1:T(8,128)(2,1)S(1)} collective-permute-done((bf16[128,32]{0,1:T(8,128)(2,1)S(1)}, bf16[128,32]{0,1:T(8,128)(2,1)S(1)}, u32[]{:S(2)}, u32[]{:S(2)}) %collective-permute-start.1) | collective-permute-done | bytes 8224 | tf_op jit(solution)/shard_map/ppermute | solution.py:21
  9.9 0.7 copy-done.2
  10.5 74.9 %tower.1 = (bf16[4,128,128]{2,1,0:T(8,128)(2,1)}, f32[5,32,128]{2,1,0:T(8,128)S(1)}, f32[96,96]{1,0:T(8,128)S(1)}, f32[96,48]{1,0:T(8,128)S(1)}, f32[32,128]{1,0:T(8,128)S(1)}) custom-call(s32[4]{0:T(128)S(1)} %bitcast.42, s32[2]{0:T(128)S(1)} %copy-done.3, s32[1]{0:T(128)} %bitcast.1.base_ref, f32[2,16,32,8]{3,2,1,0:T(8,128)S(1)} %bitcast.39, ...), custom_call_target="tpu_custom_call" | custom-call | tf_op jit(solution)/shard_map/tower/pallas_call | solution.py:197
  85.4 0.6 copy-done.1
  86.3 0.1 slice.28
  86.4 0.7 select_maximum_fusion.flat_ref
  87.1 19.6 %exchange.1 = (f32[96,128]{1,0:T(8,128)}, f32[1,32,128]{2,1,0:T(8,128)}) custom-call(f32[96,128]{1,0:T(8,128)} %select_maximum_fusion.flat_ref, f32[5,32,128]{2,1,0:T(8,128)} %copy-done.1), custom_call_target="tpu_custom_call" | custom-call | tf_op jit(solution)/shard_map/exchange/pallas_call | solution.py:392
  106.7 1.4 %slice_reduce_fusion = f32[32]{0:T(128)} fusion(f32[96,128]{1,0:T(8,128)} %get-tuple-element.17), kind=kLoop, calls=%fused_computation.15 | loop fusion | bytes 256 | tf_op jit(solution)/shard_map/slice | solution.py:438
  108.2 0.9 slice.30
  109.1 0.2 broadcast_multiply_fusion
  109.3 0.6 copy-done.5
  109.9 0.1 reshape.48
  110.1 0.2 rev.14
  110.4 0.7 copy.24
  111.2 0.6 copy.30
  (31 shorter events, 1.0 us)
Async XLA Ops:
  0.6 3.3 %copy-start.8 = (bf16[32]{0:T(256)(128)(2,1)S(1)}, bf16[32]{0:T(256)(128)(2,1)}, u32[]{:S(2)}) copy-start(bf16[32]{0:T(256)(128)(2,1)} %param.8) | copy-start | bytes 196
  0.6 9.1 %collective-permute-start = (bf16[256,32]{0,1:T(8,128)(2,1)}, bf16[256,32]{0,1:T(8,128)(2,1)S(1)}, u32[]{:S(2)}, u32[]{:S(2)}) collective-permute-start(bf16[256,32]{0,1:T(8,128)(2,1)} %param.6), channel_id=1, source_target_pairs={{2,0},{4,2},{6,4},{8,6},{10,8},{12,10},{14,12},{16,14},{18,16},{20... | collective-permute-start | bytes 49160 | tf_op jit(solution)/shard_map/ppermute | solution.py:21
  2.6 7.1 %collective-permute-start.1 = (bf16[128,32]{0,1:T(8,128)(2,1)S(1)}, bf16[128,32]{0,1:T(8,128)(2,1)S(1)}, u32[]{:S(2)}, u32[]{:S(2)}) collective-permute-start(bf16[128,32]{0,1:T(8,128)(2,1)S(1)} %slice.25), channel_id=1, source_target_pairs={{4,0},{6,2},{8,4},{10,6},{12,8},{14,10},{16,12},{18,14},{20,16},{2... | collective-permute-start | bytes 24584 | tf_op jit(solution)/shard_map/ppermute | solution.py:21
  4.0 1.0 copy-start.4
  5.3 0.7 copy-start.6
  6.6 3.3 %copy-start = (bf16[1,4,128,128]{3,2,1,0:T(8,128)(2,1)S(1)}, bf16[1,4,128,128]{3,2,1,0:T(8,128)(2,1)}, u32[]{:S(2)}) copy-start(bf16[1,4,128,128]{3,2,1,0:T(8,128)(2,1)} %param.11) | copy-start | bytes 393220
  9.9 0.7 copy-start.2
  9.9 0.7 copy-start.3
  85.4 0.6 copy-start.1
  109.1 0.8 copy-start.5
  110.4 0.8 copy-start.7
where the time goes:
time: 112 us
  Pallas kernels  94.5 us (84%)
  local copies, waits for them, and re-layouts  9.35 us (8%)
  waiting for transfers between devices  3.18 us (3%)
  starting transfers between devices  2.57 us (2%)
  other arithmetic  1.32 us (1%)
    pallas_call x1, Pallas kernels, tower(): pl.pallas_call(partial(tower_kernel, total_bins=total_bins), grid_spec=pl...  74.9 us
    pallas_call x1, Pallas kernels, exchange(): pl.pallas_call(partial(exchange_kernel, rows_n, diag_n, tile_rows, per),...  19.6 us
    unnamed x21, local copies, waits for them, and re-layouts  4.05 us
    ppermute x2, waiting for transfers between devices, shifted_2(): return lax.ppermute(block, axis, route)  3.18 us
    ppermute x2, starting transfers between devices, shifted_2(): return lax.ppermute(block, axis, route)  2.57 us
  transfers between devices with their start and end apart: 2, of which 1 were waited for; matrix products, arithmetic and copies ran while one was open for 2% of the time, Pallas kernels for 0%

commit v1 on v0

--- a/solution.py
+++ b/solution.py
@@ -81,33 +81,40 @@
     def transposed_dot(x, y):
         return lax.dot_general(x, y, (((1,), (1,)), ((), ())), preferred_element_type=jnp.float32)
 
+    def slab(ref, base):
+        return ref[pl.ds(pl.multiple_of(base, GROUP), GROUP), :]
+
     def first(g, _):
+        base = g * GROUP
         left = left_ref[0, g]
-        for j in range(GROUP):
-            p = g * GROUP + j
-            one = jnp.broadcast_to(left[:, j:j + 1], (channels, TILE))
-            pairs = 0.5 * (jnp.concatenate([one] * 3, 0) + right3_ref[...])
+        right3 = right3_ref[...]
+        cots = [slab(ref, base) for ref in (cot_b, cot_f, cot_a)]
+        ones = [jnp.broadcast_to(left[:, j:j + 1], (channels, TILE)) for j in range(GROUP)]
+        for j, one in enumerate(ones):
+            p = base + j
+            pairs = 0.5 * (jnp.concatenate([one] * 3, 0) + right3)
             pair_ref[p] = pairs[channels:2 * channels]
             a0_ref[p + DMAX] = jnp.maximum(pairs, 0.0).astype(jnp.bfloat16)
+            shown = [cot[j:j + 1] for cot in cots]
             row = jnp.where(
-                sub_c == 0, cot_b[pl.ds(p, 1), :],
-                jnp.where(sub_c == 1, cot_f[pl.ds(p, 1), :],
-                          jnp.where(sub_c == 2, cot_a[pl.ds(p, 1), :], 0.0)))
+                sub_c == 0, shown[0],
+                jnp.where(sub_c == 1, shown[1], jnp.where(sub_c == 2, shown[2], 0.0)))
             cs_ref[p + DMAX] = row.astype(jnp.bfloat16)
         return 0
 
     lax.fori_loop(0, TILE // GROUP, first, 0)
 
     def second_layer(g, _):
+        base = g * GROUP
+        values = []
         for j in range(0, GROUP, 2):
-            p = g * GROUP + j
-            at = p + DMAX
+            at = base + j + DMAX
             around = beside([column(a0_ref, at + i, d0) for i in range(2)])
             out = jnp.dot(k0_ref[...], around, preferred_element_type=jnp.float32)
-            for i in range(2):
-                value = pair_ref[p + i] + out[:, i * TILE:(i + 1) * TILE]
-                pair1_ref[p + i] = value
-                put(a1_ref, p + i, jnp.maximum(value, 0.0), d1)
+            values += [pair_ref[base + j + i] + out[:, i * TILE:(i + 1) * TILE] for i in range(2)]
+        for j, value in enumerate(values):
+            pair1_ref[base + j] = value
+            put(a1_ref, base + j, jnp.maximum(value, 0.0), d1)
         return 0
 
     lax.fori_loop(0, TILE // GROUP, second_layer, 0)
@@ -117,7 +124,8 @@
     def turn(g, carry):
         acc_u, acc_h = carry
         base = g * GROUP
-        rows = []
+        cots = slab(cot_f, base)
+        rows, grads = [], []
         for j in range(0, GROUP, 2):
             p = base + j
             at = p + DMAX
@@ -125,17 +133,19 @@
             out = jnp.dot(k1_ref[...], around, preferred_element_type=jnp.float32)
             for i in range(2):
                 value = pair1_ref[p + i]
-                cot = cot_f[pl.ds(p + i, 1), :]
+                cot = cots[j + i:j + i + 1]
                 pair2 = value + out[:channels, i * TILE:(i + 1) * TILE]
                 rows.append(jnp.sum(head * pair2, 0, keepdims=True))
                 acc_h = acc_h + pair2 * cot
-                grad = head * cot + jnp.where(value > 0.0, out[channels:, i * TILE:(i + 1) * TILE], 0.0)
-                pair_ref[p + i] = grad
-                put(gs_ref, p + i, grad, d0)
-        pred_f[pl.ds(pl.multiple_of(base, GROUP), GROUP), :] = jnp.concatenate(rows, 0)
+                grads.append(
+                    head * cot + jnp.where(value > 0.0, out[channels:, i * TILE:(i + 1) * TILE], 0.0))
         every = [base + DMAX + j for j in range(GROUP)]
         acc_u = acc_u + transposed_dot(
             beside([[a1_ref[at]] for at in every]), beside([column(cs_ref, at, d1) for at in every]))
+        for j, grad in enumerate(grads):
+            pair_ref[base + j] = grad
+            put(gs_ref, base + j, grad, d0)
+        pred_f[pl.ds(pl.multiple_of(base, GROUP), GROUP), :] = jnp.concatenate(rows, 0)
         return acc_u, acc_h
 
     acc_u, acc_h = lax.fori_loop(
@@ -148,6 +158,11 @@
     def last(g, carry):
         grad_left, grad_right = carry
         base = g * GROUP
+        every = [base + DMAX + j for j in range(GROUP)]
+        grad_k = transposed_dot(
+            beside([[a0_ref[at]] for at in every]),
+            beside([[gs_ref[at - d0, mid], gs_ref[at, mid], gs_ref[at + d0, mid]] for at in every]))
+        sums = []
         for j in range(0, GROUP, 2):
             p = base + j
             at = p + DMAX
@@ -157,11 +172,10 @@
                 active = a0_ref[at + i, mid].astype(jnp.float32) > 0.0
                 grad = pair_ref[p + i] + jnp.where(active, out[:, i * TILE:(i + 1) * TILE], 0.0)
                 grad_right = grad_right + grad
-                grad_left = jnp.where(lane == p + i, jnp.sum(grad, 1, keepdims=True), grad_left)
-        every = [base + DMAX + j for j in range(GROUP)]
-        gk0_ref[...] += transposed_dot(
-            beside([[a0_ref[at]] for at in every]),
-            beside([[gs_ref[at - d0, mid], gs_ref[at, mid], gs_ref[at + d0, mid]] for at in every]))
+                sums.append(jnp.sum(grad, 1, keepdims=True))
+        for j, total in enumerate(sums):
+            grad_left = jnp.where(lane == base + j, total, grad_left)
+        gk0_ref[...] += grad_k
         return grad_left, grad_right
 
     zeros = jnp.zeros((channels, TILE), jnp.float32)

time: 112 us -> 115 us (1.027)
  Pallas kernels: 94.5 us -> 97.5 us
    pallas_call x1, Pallas kernels: 74.9 us -> 77.8 us  [tower(): pl.pallas_call(partial(tower_kernel, total_bins=total_bins), grid_spec=pl...]
where the time goes in v1:
time: 115 us
  Pallas kernels  97.5 us (85%)
  local copies, waits for them, and re-layouts  9.35 us (8%)
  waiting for transfers between devices  3.18 us (3%)
  starting transfers between devices  2.57 us (2%)
  other arithmetic  1.32 us (1%)
    pallas_call x1, Pallas kernels, tower(): pl.pallas_call(partial(tower_kernel, total_bins=total_bins), grid_spec=pl...  77.8 us
    pallas_call x1, Pallas kernels, exchange(): pl.pallas_call(partial(exchange_kernel, rows_n, diag_n, tile_rows, per),...  19.7 us
    unnamed x21, local copies, waits for them, and re-layouts  4.05 us
    ppermute x2, waiting for transfers between devices, shifted_2(): return lax.ppermute(block, axis, route)  3.18 us
    ppermute x2, starting transfers between devices, shifted_2(): return lax.ppermute(block, axis, route)  2.57 us
  transfers between devices with their start and end apart: 2, of which 1 were waited for; matrix products, arithmetic and copies ran while one was open for 2% of the time, Pallas kernels for 0%

profile of v1, /device:TPU:0, one launch (start us, length us, event | category | flops | bytes accessed | tf_op | source)
XLA Modules:
  0.0 114.7 jit_solution(2556892407667729127)
XLA Ops:
  0.6 1.3 %collective-permute-start = (bf16[256,32]{0,1:T(8,128)(2,1)}, bf16[256,32]{0,1:T(8,128)(2,1)S(1)}, u32[]{:S(2)}, u32[]{:S(2)}) collective-permute-start(bf16[256,32]{0,1:T(8,128)(2,1)} %param.6), channel_id=1, source_target_pairs={{2,0},{4,2},{6,4},{8,6},{10,8},{12,10},{14,12},{16,14},{18,16},{20... | collective-permute-start | bytes 49160 | tf_op jit(solution)/shard_map/ppermute | solution.py:21
  1.9 0.7 slice.25
  2.6 1.3 %collective-permute-start.1 = (bf16[128,32]{0,1:T(8,128)(2,1)S(1)}, bf16[128,32]{0,1:T(8,128)(2,1)S(1)}, u32[]{:S(2)}, u32[]{:S(2)}) collective-permute-start(bf16[128,32]{0,1:T(8,128)(2,1)S(1)} %slice.25), channel_id=1, source_target_pairs={{4,0},{6,2},{8,4},{10,6},{12,8},{14,10},{16,12},{18,14},{20,16},{2... | collective-permute-start | bytes 24584 | tf_op jit(solution)/shard_map/ppermute | solution.py:21
  4.0 1.0 fusion.4
  4.9 0.1 fusion
  5.4 0.6 copy-done.6
  6.0 0.1 copy.16
  6.3 0.1 reshape.46.k0t_ref
  6.4 0.1 copy.17
  6.6 3.2 %collective-permute-done.1 = bf16[128,32]{0,1:T(8,128)(2,1)S(1)} collective-permute-done((bf16[128,32]{0,1:T(8,128)(2,1)S(1)}, bf16[128,32]{0,1:T(8,128)(2,1)S(1)}, u32[]{:S(2)}, u32[]{:S(2)}) %collective-permute-start.1) | collective-permute-done | bytes 8224 | tf_op jit(solution)/shard_map/ppermute | solution.py:21
  9.9 0.7 copy-done.2
  10.5 77.8 %tower.1 = (bf16[4,128,128]{2,1,0:T(8,128)(2,1)}, f32[5,32,128]{2,1,0:T(8,128)S(1)}, f32[96,96]{1,0:T(8,128)S(1)}, f32[96,48]{1,0:T(8,128)S(1)}, f32[32,128]{1,0:T(8,128)S(1)}) custom-call(s32[4]{0:T(128)S(1)} %bitcast.42, s32[2]{0:T(128)S(1)} %copy-done.3, s32[1]{0:T(128)} %bitcast.1.base_ref, f32[2,16,32,8]{3,2,1,0:T(8,128)S(1)} %bitcast.39, ...), custom_call_target="tpu_custom_call" | custom-call | tf_op jit(solution)/shard_map/tower/pallas_call | solution.py:211
  88.3 0.6 copy-done.1
  89.2 0.1 slice.28
  89.3 0.7 select_maximum_fusion.flat_ref
  90.0 19.7 %exchange.1 = (f32[96,128]{1,0:T(8,128)}, f32[1,32,128]{2,1,0:T(8,128)}) custom-call(f32[96,128]{1,0:T(8,128)} %select_maximum_fusion.flat_ref, f32[5,32,128]{2,1,0:T(8,128)} %copy-done.1), custom_call_target="tpu_custom_call" | custom-call | tf_op jit(solution)/shard_map/exchange/pallas_call | solution.py:406
  109.7 1.4 %slice_reduce_fusion = f32[32]{0:T(128)} fusion(f32[96,128]{1,0:T(8,128)} %get-tuple-element.17), kind=kLoop, calls=%fused_computation.15 | loop fusion | bytes 256 | tf_op jit(solution)/shard_map/slice | solution.py:452
  111.1 0.9 slice.30
  112.1 0.2 broadcast_multiply_fusion
  112.3 0.6 copy-done.5
  112.9 0.1 reshape.48
  113.0 0.2 rev.14
  113.4 0.7 copy.24
  114.1 0.6 copy.30
  (31 shorter events, 1.0 us)
Async XLA Ops:
  0.6 3.3 %copy-start.8 = (bf16[32]{0:T(256)(128)(2,1)S(1)}, bf16[32]{0:T(256)(128)(2,1)}, u32[]{:S(2)}) copy-start(bf16[32]{0:T(256)(128)(2,1)} %param.8) | copy-start | bytes 196
  0.6 9.1 %collective-permute-start = (bf16[256,32]{0,1:T(8,128)(2,1)}, bf16[256,32]{0,1:T(8,128)(2,1)S(1)}, u32[]{:S(2)}, u32[]{:S(2)}) collective-permute-start(bf16[256,32]{0,1:T(8,128)(2,1)} %param.6), channel_id=1, source_target_pairs={{2,0},{4,2},{6,4},{8,6},{10,8},{12,10},{14,12},{16,14},{18,16},{20... | collective-permute-start | bytes 49160 | tf_op jit(solution)/shard_map/ppermute | solution.py:21
  2.6 7.1 %collective-permute-start.1 = (bf16[128,32]{0,1:T(8,128)(2,1)S(1)}, bf16[128,32]{0,1:T(8,128)(2,1)S(1)}, u32[]{:S(2)}, u32[]{:S(2)}) collective-permute-start(bf16[128,32]{0,1:T(8,128)(2,1)S(1)} %slice.25), channel_id=1, source_target_pairs={{4,0},{6,2},{8,4},{10,6},{12,8},{14,10},{16,12},{18,14},{20,16},{2... | collective-permute-start | bytes 24584 | tf_op jit(solution)/shard_map/ppermute | solution.py:21
  4.0 1.0 copy-start.4
  5.3 0.7 copy-start.6
  6.6 3.3 %copy-start = (bf16[1,4,128,128]{3,2,1,0:T(8,128)(2,1)S(1)}, bf16[1,4,128,128]{3,2,1,0:T(8,128)(2,1)}, u32[]{:S(2)}) copy-start(bf16[1,4,128,128]{3,2,1,0:T(8,128)(2,1)} %param.11) | copy-start | bytes 393220
  9.9 0.7 copy-start.2
  9.9 0.7 copy-start.3
  88.3 0.6 copy-start.1
  112.1 0.8 copy-start.5
  113.4 0.8 copy-start.7

commit v2 on v0

--- a/solution.py
+++ b/solution.py
@@ -29,7 +29,7 @@
 
 def tower_kernel(
     tiles_ref, dil_ref, base_ref,
-    left_ref, right_ref, cot_ref, k0_ref, k1_ref, k0t_ref, head_ref,
+    left_ref, right_ref, cot_ref, k0_ref, k0n_ref, k1_ref, k1n_ref, k0t_ref, k0tn_ref, w1_ref, head_ref,
     pred_ref, gwin_ref, gk0_ref, u1_ref, gh_ref,
     a0_ref, a1_ref, gs_ref, cs_ref, pair_ref, pair1_ref, right3_ref, cot_f, cot_b, cot_a, pred_f,
     *, total_bins,
@@ -81,6 +81,23 @@
     def transposed_dot(x, y):
         return lax.dot_general(x, y, (((1,), (1,)), ((), ())), preferred_element_type=jnp.float32)
 
+    def heads_of(ref, base, spacing):
+        heads, ninth = [], []
+        for j in range(0, GROUP, 2):
+            rows = [base + DMAX + j + i for i in range(2)]
+            heads.append(beside([
+                [ref[at - spacing], ref[at], ref[at + spacing, :2 * channels]] for at in rows]))
+            ninth.append(beside([[ref[at + spacing, 2 * channels:]] for at in rows]))
+        return heads, jnp.concatenate(ninth, 0)
+
+    def taps_of(ref, base, spacing, kernel_ref, ninth_ref):
+        heads, ninth = heads_of(ref, base, spacing)
+        rest = jnp.dot(ninth_ref[...], ninth, preferred_element_type=jnp.float32)
+        return [
+            rest[k * channels:(k + 1) * channels]
+            + jnp.dot(kernel_ref[...], part, preferred_element_type=jnp.float32)
+            for k, part in enumerate(heads)]
+
     def first(g, _):
         left = left_ref[0, g]
         for j in range(GROUP):
@@ -99,11 +116,10 @@
     lax.fori_loop(0, TILE // GROUP, first, 0)
 
     def second_layer(g, _):
+        outs = taps_of(a0_ref, g * GROUP, d0, k0_ref, k0n_ref)
         for j in range(0, GROUP, 2):
             p = g * GROUP + j
-            at = p + DMAX
-            around = beside([column(a0_ref, at + i, d0) for i in range(2)])
-            out = jnp.dot(k0_ref[...], around, preferred_element_type=jnp.float32)
+            out = outs[j // 2]
             for i in range(2):
                 value = pair_ref[p + i] + out[:, i * TILE:(i + 1) * TILE]
                 pair1_ref[p + i] = value
@@ -118,18 +134,22 @@
         acc_u, acc_h = carry
         base = g * GROUP
         rows = []
+        outs = taps_of(a1_ref, base, d1, k1_ref, k1n_ref)
+        cots = jnp.concatenate([
+            beside([column(cs_ref, base + DMAX + j + i, d1) for i in range(2)])
+            for j in range(0, GROUP, 2)], 0)
+        backs = jnp.dot(w1_ref[...], cots, preferred_element_type=jnp.float32)
         for j in range(0, GROUP, 2):
             p = base + j
-            at = p + DMAX
-            around = beside([column(a1_ref, at + i, d1) + column(cs_ref, at + i, d1) for i in range(2)])
-            out = jnp.dot(k1_ref[...], around, preferred_element_type=jnp.float32)
+            out = outs[j // 2]
+            back = backs[j // 2 * channels:(j // 2 + 1) * channels]
             for i in range(2):
                 value = pair1_ref[p + i]
                 cot = cot_f[pl.ds(p + i, 1), :]
-                pair2 = value + out[:channels, i * TILE:(i + 1) * TILE]
+                pair2 = value + out[:, i * TILE:(i + 1) * TILE]
                 rows.append(jnp.sum(head * pair2, 0, keepdims=True))
                 acc_h = acc_h + pair2 * cot
-                grad = head * cot + jnp.where(value > 0.0, out[channels:, i * TILE:(i + 1) * TILE], 0.0)
+                grad = head * cot + jnp.where(value > 0.0, back[:, i * TILE:(i + 1) * TILE], 0.0)
                 pair_ref[p + i] = grad
                 put(gs_ref, p + i, grad, d0)
         pred_f[pl.ds(pl.multiple_of(base, GROUP), GROUP), :] = jnp.concatenate(rows, 0)
@@ -148,11 +168,11 @@
     def last(g, carry):
         grad_left, grad_right = carry
         base = g * GROUP
+        outs = taps_of(gs_ref, base, d0, k0t_ref, k0tn_ref)
         for j in range(0, GROUP, 2):
             p = base + j
             at = p + DMAX
-            around = beside([column(gs_ref, at + i, d0) for i in range(2)])
-            out = jnp.dot(k0t_ref[...], around, preferred_element_type=jnp.float32)
+            out = outs[j // 2]
             for i in range(2):
                 active = a0_ref[at + i, mid].astype(jnp.float32) > 0.0
                 grad = pair_ref[p + i] + jnp.where(active, out[:, i * TILE:(i + 1) * TILE], 0.0)
@@ -187,8 +207,16 @@
     folded = jnp.sum(conv_weight[1].astype(f32) * head_f, -1)[::-1, ::-1]
     w1 = jnp.pad(folded, ((0, 0), (0, 13), (0, 0))).transpose(2, 0, 1).reshape(channels, 48).astype(bf16)
     k1 = conv_weight[1].reshape(taps, channels).T
-    k1 = jnp.concatenate([jnp.pad(k1, ((0, 0), (0, 48))), jnp.pad(w1, ((0, 0), (taps, 0)))], 0)
-    head_b = jnp.broadcast_to(head_f[:, None], (channels, TILE))
+    repeat = jnp.eye(GROUP // 2, dtype=bf16)
+
+    def diagonal(block):
+        size = (GROUP // 2 * block.shape[0], GROUP // 2 * block.shape[1])
+        return (repeat[:, None, :, None] * block[None, :, None, :]).reshape(size)
+
+    kernels = []
+    for kernel in (k0, k1, k0t):
+        kernels += [kernel[:, :8 * channels], diagonal(kernel[:, 8 * channels:])]
+    kernels += [diagonal(w1), jnp.broadcast_to(head_f[:, None], (channels, TILE))]
 
     def whole(shape):
         return pl.BlockSpec(shape, lambda s, *_: (0,) * len(shape))
@@ -203,7 +231,7 @@
                 pl.BlockSpec((1, TILE // GROUP, channels, GROUP), lambda s, t, d, b: (t[s] // OFFS, 0, 0, 0)),
                 pl.BlockSpec((1, channels, TILE), lambda s, t, d, b: (t[s] // OFFS + t[s] % OFFS, 0, 0)),
                 pl.BlockSpec((1, TILE, TILE), lambda s, t, d, b: (s, 0, 0)),
-                whole(k0.shape), whole(k1.shape), whole(k0t.shape), whole(head_b.shape),
+                *[whole(kernel.shape) for kernel in kernels],
             ],
             out_specs=[
                 pl.BlockSpec((1, TILE, TILE), lambda s, t, d, b: (s, 0, 0)),
@@ -236,7 +264,7 @@
         compiler_params=pltpu.CompilerParams(
             dimension_semantics=("arbitrary",), vmem_limit_bytes=40 * 1024 * 1024),
         name="tower",
-    )(tiles, dilation, base_row, left, right, cotangent, k0, k1, k0t, head_b)
+    )(tiles, dilation, base_row, left, right, cotangent, *kernels)
     return outs
 
 

time: 112 us -> 108 us (0.964)
  Pallas kernels: 94.5 us -> 90.5 us
    pallas_call x1, Pallas kernels: 74.9 us -> 70.4 us  [tower(): pl.pallas_call(partial(tower_kernel, total_bins=total_bins), grid_spec=pl...]
  transfers between devices with their start and end apart: 2 -> 2, of which waited for: 1 -> 1; matrix products, arithmetic and copies ran while one was open for 2% -> 3% of each run, Pallas kernels for 0% -> 0%
where the time goes in v2:
time: 108 us
  Pallas kernels  90.5 us (84%)
  local copies, waits for them, and re-layouts  9.81 us (9%)
  starting transfers between devices  2.7 us (2%)
  waiting for transfers between devices  2.37 us (2%)
  other arithmetic  1.58 us (1%)
    pallas_call x1, Pallas kernels, tower(): pl.pallas_call(partial(tower_kernel, total_bins=total_bins), grid_spec=pl...  70.4 us
    pallas_call x1, Pallas kernels, exchange(): pl.pallas_call(partial(exchange_kernel, rows_n, diag_n, tile_rows, per),...  20.1 us
    unnamed x21, local copies, waits for them, and re-layouts  4 us
    ppermute x2, starting transfers between devices, shifted_2(): return lax.ppermute(block, axis, route)  2.7 us
    ppermute x2, waiting for transfers between devices, shifted_2(): return lax.ppermute(block, axis, route)  2.37 us
  transfers between devices with their start and end apart: 2, of which 1 were waited for; matrix products, arithmetic and copies ran while one was open for 3% of the time, Pallas kernels for 0%

profile of v2, /device:TPU:0, one launch (start us, length us, event | category | flops | bytes accessed | tf_op | source)
XLA Modules:
  0.0 107.9 jit_solution(2732239069897922134)
XLA Ops:
  0.6 1.3 %collective-permute-start = (bf16[256,32]{0,1:T(8,128)(2,1)}, bf16[256,32]{0,1:T(8,128)(2,1)S(1)}, u32[]{:S(2)}, u32[]{:S(2)}) collective-permute-start(bf16[256,32]{0,1:T(8,128)(2,1)} %param.6), channel_id=1, source_target_pairs={{2,0},{4,2},{6,4},{8,6},{10,8},{12,10},{14,12},{16,14},{18,16},{20... | collective-permute-start | bytes 49160 | tf_op jit(solution)/shard_map/ppermute | solution.py:21
  1.9 0.7 slice.43
  2.6 1.4 %collective-permute-start.1 = (bf16[128,32]{0,1:T(8,128)(2,1)S(1)}, bf16[128,32]{0,1:T(8,128)(2,1)S(1)}, u32[]{:S(2)}, u32[]{:S(2)}) collective-permute-start(bf16[128,32]{0,1:T(8,128)(2,1)S(1)} %slice.43), channel_id=1, source_target_pairs={{4,0},{6,2},{8,4},{10,6},{12,8},{14,10},{16,12},{18,14},{20,16},{2... | collective-permute-start | bytes 24584 | tf_op jit(solution)/shard_map/ppermute | solution.py:21
  4.1 1.0 fusion.2
  5.7 0.2 broadcast_multiply_fusion.2
  6.1 0.6 copy-done.6
  6.8 0.1 mul.115.w1_ref
  7.0 0.1 mul.109.k0tn_ref
  7.1 0.1 mul.106.k1n_ref
  7.4 0.1 copy.17
  7.5 2.4 %collective-permute-done.1 = bf16[128,32]{0,1:T(8,128)(2,1)S(1)} collective-permute-done((bf16[128,32]{0,1:T(8,128)(2,1)S(1)}, bf16[128,32]{0,1:T(8,128)(2,1)S(1)}, u32[]{:S(2)}, u32[]{:S(2)}) %collective-permute-start.1) | collective-permute-done | bytes 8224 | tf_op jit(solution)/shard_map/ppermute | solution.py:21
  10.0 0.7 copy-done.2
  10.7 70.4 %tower.1 = (bf16[4,128,128]{2,1,0:T(8,128)(2,1)}, f32[5,32,128]{2,1,0:T(8,128)S(1)}, f32[96,96]{1,0:T(8,128)S(1)}, f32[96,48]{1,0:T(8,128)S(1)}, f32[32,128]{1,0:T(8,128)S(1)}) custom-call(s32[4]{0:T(128)S(1)} %bitcast.41, s32[2]{0:T(128)S(1)} %copy-done.3, s32[1]{0:T(128)} %bitcast.1.base_ref, f32[2,16,32,8]{3,2,1,0:T(8,128)S(1)} %bitcast.39, ...), custom_call_target="tpu_custom_call" | custom-call | tf_op jit(solution)/shard_map/tower/pallas_call | solution.py:225
  81.0 0.6 copy-done.1
  82.0 0.7 select_maximum_fusion.flat_ref
  82.7 20.1 %exchange.1 = (f32[96,128]{1,0:T(8,128)}, f32[1,32,128]{2,1,0:T(8,128)}) custom-call(f32[96,128]{1,0:T(8,128)} %select_maximum_fusion.flat_ref, f32[5,32,128]{2,1,0:T(8,128)} %copy-done.1), custom_call_target="tpu_custom_call" | custom-call | tf_op jit(solution)/shard_map/exchange/pallas_call | solution.py:420
  102.9 1.4 %slice_reduce_fusion = f32[32]{0:T(128)} fusion(f32[96,128]{1,0:T(8,128)} %get-tuple-element.17), kind=kLoop, calls=%fused_computation.14 | loop fusion | bytes 256 | tf_op jit(solution)/shard_map/slice | solution.py:466
  104.3 0.9 slice.54
  105.2 0.2 broadcast_multiply_fusion
  105.4 0.6 copy-done.5
  106.0 0.1 reshape.80
  106.2 0.2 rev.14
  106.5 0.7 copy.24
  107.3 0.6 copy.30
  (43 shorter events, 1.6 us)
Async XLA Ops:
  0.6 9.3 %collective-permute-start = (bf16[256,32]{0,1:T(8,128)(2,1)}, bf16[256,32]{0,1:T(8,128)(2,1)S(1)}, u32[]{:S(2)}, u32[]{:S(2)}) collective-permute-start(bf16[256,32]{0,1:T(8,128)(2,1)} %param.6), channel_id=1, source_target_pairs={{2,0},{4,2},{6,4},{8,6},{10,8},{12,10},{14,12},{16,14},{18,16},{20... | collective-permute-start | bytes 49160 | tf_op jit(solution)/shard_map/ppermute | solution.py:21
  2.6 1.4 %copy-start.8 = (bf16[32]{0:T(256)(128)(2,1)S(1)}, bf16[32]{0:T(256)(128)(2,1)}, u32[]{:S(2)}) copy-start(bf16[32]{0:T(256)(128)(2,1)} %param.8) | copy-start | bytes 196
  2.6 7.3 %collective-permute-start.1 = (bf16[128,32]{0,1:T(8,128)(2,1)S(1)}, bf16[128,32]{0,1:T(8,128)(2,1)S(1)}, u32[]{:S(2)}, u32[]{:S(2)}) collective-permute-start(bf16[128,32]{0,1:T(8,128)(2,1)S(1)} %slice.43), channel_id=1, source_target_pairs={{4,0},{6,2},{8,4},{10,6},{12,8},{14,10},{16,12},{18,14},{20,16},{2... | collective-permute-start | bytes 24584 | tf_op jit(solution)/shard_map/ppermute | solution.py:21
  4.1 1.0 copy-start.4
  6.0 0.7 copy-start.6
  7.5 2.5 %copy-start = (bf16[1,4,128,128]{3,2,1,0:T(8,128)(2,1)S(1)}, bf16[1,4,128,128]{3,2,1,0:T(8,128)(2,1)}, u32[]{:S(2)}) copy-start(bf16[1,4,128,128]{3,2,1,0:T(8,128)(2,1)} %param.11) | copy-start | bytes 393220
  10.0 0.7 copy-start.2
  10.0 0.7 copy-start.3
  81.0 0.6 copy-start.1
  105.2 0.8 copy-start.5
  106.5 0.8 copy-start.7

commit v3 on v2

--- a/solution.py
+++ b/solution.py
@@ -330,8 +330,7 @@
             device_id=device, device_id_type=mesh_id)
 
     def sum_copy(step, slot, axis, e):
-        src = flat_ref if step == 0 else part_ref.at[step - 1]
-        return remote(src, got_ref.at[slot], sum_send.at[slot], sum_recv.at[slot], partner(axis, e))
+        return remote(part_ref.at[step], got_ref.at[slot], sum_send.at[slot], sum_recv.at[slot], partner(axis, e))
 
     def own_copy(e):
         src = gwin_ref.at[pl.ds(start_of(d ^ e), count)]
@@ -357,8 +356,8 @@
     value = flat_ref[...]
     copies = []
     for step, (axis, group) in enumerate(steps):
-        if step > 0:
-            part_ref[step - 1] = value
+        part_ref[step] = value.astype(jnp.bfloat16)
+        value = part_ref[step].astype(jnp.float32)
         here = [sum_copy(step, slot + i, axis, e) for i, e in enumerate(group)]
         for copy in here:
             copy.start()
@@ -370,7 +369,7 @@
                 pl.when(sends_far(e))(far_copy(e).start)
         for copy in here:
             copy.wait_recv()
-        others = [got_ref[slot + i] for i in range(len(group))]
+        others = [got_ref[slot + i].astype(jnp.float32) for i in range(len(group))]
         value = value + others[0]
         if len(group) == 3:
             value = value + (others[1] + others[2])
@@ -423,8 +422,8 @@
         in_specs=[vmem] * 2,
         out_specs=[vmem] * 2,
         scratch_shapes=[
-            pltpu.VMEM((len(steps),) + flat.shape, f32),
-            pltpu.VMEM((slots,) + flat.shape, f32),
+            pltpu.VMEM((len(steps),) + flat.shape, bf16),
+            pltpu.VMEM((slots,) + flat.shape, bf16),
             pltpu.VMEM((tile_rows,) + block, bf16),
             pltpu.VMEM(block, bf16),
             pltpu.VMEM((others, count) + block, f32),

time: 108 us -> 105 us (0.972)
  Pallas kernels: 90.5 us -> 87.6 us
    pallas_call x1, Pallas kernels: 20.1 us -> 17.4 us  [exchange(): pl.pallas_call(partial(exchange_kernel, rows_n, diag_n, tile_rows, per),...]
where the time goes in v3:
time: 105 us
  Pallas kernels  87.6 us (83%)
  local copies, waits for them, and re-layouts  9.81 us (9%)
  starting transfers between devices  2.7 us (3%)
  waiting for transfers between devices  2.37 us (2%)
  other arithmetic  1.58 us (2%)
    pallas_call x1, Pallas kernels, tower(): pl.pallas_call(partial(tower_kernel, total_bins=total_bins), grid_spec=pl...  70.2 us
    pallas_call x1, Pallas kernels, exchange(): pl.pallas_call(partial(exchange_kernel, rows_n, diag_n, tile_rows, per),...  17.4 us
    unnamed x21, local copies, waits for them, and re-layouts  4 us
    ppermute x2, starting transfers between devices, shifted_2(): return lax.ppermute(block, axis, route)  2.7 us
    ppermute x2, waiting for transfers between devices, shifted_2(): return lax.ppermute(block, axis, route)  2.37 us
  transfers between devices with their start and end apart: 2, of which 1 were waited for; matrix products, arithmetic and copies ran while one was open for 3% of the time, Pallas kernels for 0%

profile of v3, /device:TPU:0, one launch (start us, length us, event | category | flops | bytes accessed | tf_op | source)
XLA Modules:
  0.0 105.0 jit_solution(14836322101225446286)
XLA Ops:
  0.6 1.3 %collective-permute-start = (bf16[256,32]{0,1:T(8,128)(2,1)}, bf16[256,32]{0,1:T(8,128)(2,1)S(1)}, u32[]{:S(2)}, u32[]{:S(2)}) collective-permute-start(bf16[256,32]{0,1:T(8,128)(2,1)} %param.6), channel_id=1, source_target_pairs={{2,0},{4,2},{6,4},{8,6},{10,8},{12,10},{14,12},{16,14},{18,16},{20... | collective-permute-start | bytes 49160 | tf_op jit(solution)/shard_map/ppermute | solution.py:21
  1.9 0.7 slice.43
  2.6 1.4 %collective-permute-start.1 = (bf16[128,32]{0,1:T(8,128)(2,1)S(1)}, bf16[128,32]{0,1:T(8,128)(2,1)S(1)}, u32[]{:S(2)}, u32[]{:S(2)}) collective-permute-start(bf16[128,32]{0,1:T(8,128)(2,1)S(1)} %slice.43), channel_id=1, source_target_pairs={{4,0},{6,2},{8,4},{10,6},{12,8},{14,10},{16,12},{18,14},{20,16},{2... | collective-permute-start | bytes 24584 | tf_op jit(solution)/shard_map/ppermute | solution.py:21
  4.1 1.0 fusion.2
  5.7 0.2 broadcast_multiply_fusion.2
  6.1 0.6 copy-done.6
  6.8 0.1 mul.115.w1_ref
  7.0 0.1 mul.109.k0tn_ref
  7.1 0.1 mul.106.k1n_ref
  7.4 0.1 copy.17
  7.5 2.4 %collective-permute-done.1 = bf16[128,32]{0,1:T(8,128)(2,1)S(1)} collective-permute-done((bf16[128,32]{0,1:T(8,128)(2,1)S(1)}, bf16[128,32]{0,1:T(8,128)(2,1)S(1)}, u32[]{:S(2)}, u32[]{:S(2)}) %collective-permute-start.1) | collective-permute-done | bytes 8224 | tf_op jit(solution)/shard_map/ppermute | solution.py:21
  10.0 0.7 copy-done.2
  10.7 70.2 %tower.1 = (bf16[4,128,128]{2,1,0:T(8,128)(2,1)}, f32[5,32,128]{2,1,0:T(8,128)S(1)}, f32[96,96]{1,0:T(8,128)S(1)}, f32[96,48]{1,0:T(8,128)S(1)}, f32[32,128]{1,0:T(8,128)S(1)}) custom-call(s32[4]{0:T(128)S(1)} %bitcast.41, s32[2]{0:T(128)S(1)} %copy-done.3, s32[1]{0:T(128)} %bitcast.1.base_ref, f32[2,16,32,8]{3,2,1,0:T(8,128)S(1)} %bitcast.39, ...), custom_call_target="tpu_custom_call" | custom-call | tf_op jit(solution)/shard_map/tower/pallas_call | solution.py:225
  80.8 0.6 copy-done.1
  81.8 0.7 select_maximum_fusion.flat_ref
  82.5 17.4 %exchange.1 = (f32[96,128]{1,0:T(8,128)}, f32[1,32,128]{2,1,0:T(8,128)}) custom-call(f32[96,128]{1,0:T(8,128)} %select_maximum_fusion.flat_ref, f32[5,32,128]{2,1,0:T(8,128)} %copy-done.1), custom_call_target="tpu_custom_call" | custom-call | tf_op jit(solution)/shard_map/exchange/pallas_call | solution.py:419
  100.0 1.4 %slice_reduce_fusion = f32[32]{0:T(128)} fusion(f32[96,128]{1,0:T(8,128)} %get-tuple-element.17), kind=kLoop, calls=%fused_computation.14 | loop fusion | bytes 256 | tf_op jit(solution)/shard_map/slice | solution.py:465
  101.4 0.9 slice.54
  102.3 0.2 broadcast_multiply_fusion
  102.5 0.6 copy-done.5
  103.1 0.1 reshape.80
  103.3 0.2 rev.14
  103.6 0.7 copy.24
  104.4 0.6 copy.30
  (43 shorter events, 1.6 us)
Async XLA Ops:
  0.6 9.3 %collective-permute-start = (bf16[256,32]{0,1:T(8,128)(2,1)}, bf16[256,32]{0,1:T(8,128)(2,1)S(1)}, u32[]{:S(2)}, u32[]{:S(2)}) collective-permute-start(bf16[256,32]{0,1:T(8,128)(2,1)} %param.6), channel_id=1, source_target_pairs={{2,0},{4,2},{6,4},{8,6},{10,8},{12,10},{14,12},{16,14},{18,16},{20... | collective-permute-start | bytes 49160 | tf_op jit(solution)/shard_map/ppermute | solution.py:21
  2.6 1.4 %copy-start.8 = (bf16[32]{0:T(256)(128)(2,1)S(1)}, bf16[32]{0:T(256)(128)(2,1)}, u32[]{:S(2)}) copy-start(bf16[32]{0:T(256)(128)(2,1)} %param.8) | copy-start | bytes 196
  2.6 7.3 %collective-permute-start.1 = (bf16[128,32]{0,1:T(8,128)(2,1)S(1)}, bf16[128,32]{0,1:T(8,128)(2,1)S(1)}, u32[]{:S(2)}, u32[]{:S(2)}) collective-permute-start(bf16[128,32]{0,1:T(8,128)(2,1)S(1)} %slice.43), channel_id=1, source_target_pairs={{4,0},{6,2},{8,4},{10,6},{12,8},{14,10},{16,12},{18,14},{20,16},{2... | collective-permute-start | bytes 24584 | tf_op jit(solution)/shard_map/ppermute | solution.py:21
  4.1 1.0 copy-start.4
  6.0 0.7 copy-start.6
  7.5 2.5 %copy-start = (bf16[1,4,128,128]{3,2,1,0:T(8,128)(2,1)S(1)}, bf16[1,4,128,128]{3,2,1,0:T(8,128)(2,1)}, u32[]{:S(2)}) copy-start(bf16[1,4,128,128]{3,2,1,0:T(8,128)(2,1)} %param.11) | copy-start | bytes 393220
  10.0 0.7 copy-start.2
  10.0 0.7 copy-start.3
  80.8 0.6 copy-start.1
  102.3 0.8 copy-start.5
  103.6 0.8 copy-start.7
